TPU v7x, 512 devices: a whole 4x8x8 slice. The times are simulated.
512 devices in a mesh: dp: 4 (over x), trow: 16 (over y_lo, z), tcol: 8 (over y_hi, core).
Axes of the slice: x: 4, y: 8 (y_hi: 4, y_lo: 2; y = y_hi * 2 + y_lo), z: 8, core: 2. Of those that a mesh axis runs over, the one named last changes fastest.
Arguments:
- gate: bfloat16 [4, 16384, 256], P('dp', ('trow', 'tcol')), may hold values from -6 to 6
- value: bfloat16 [4, 16384, 256], P('dp', ('trow', 'tcol')), may hold values from -6 to 6
- grad_out: bfloat16 [4, 16384, 256], P('dp', ('trow', 'tcol')), may hold values from -6 to 6
- filter_raw: float32 [16384, 256], P(('trow', 'tcol')), may hold values from -6 to 6
Outputs:
- grad_gate: bfloat16 [4, 16384, 256], P('dp', ('trow', 'tcol'))
- grad_value: bfloat16 [4, 16384, 256], P('dp', ('trow', 'tcol'))
- grad_filter: float32 [16384, 256], P(('trow', 'tcol'), 'dp')
All inputs are finite; a program needn't handle non-finite values.
Results may differ from a plain program's by a relative error of at most 0.001.
Values sent between devices are 32-bit elements; how exact they have to be, the bound alone decides.
A program may use at most 64 MiB of HBM per device.

v0:
```python
import math

import jax
import jax.numpy as jnp
from jax import lax
from jax.sharding import PartitionSpec as P

CB = 1


PRECISE = lax.Precision.HIGHEST


def count_up(length):
    return jnp.arange(length, dtype=jnp.int32)


def angles(first, second, period):
    product = first[:, None] * second[None, :] % period
    theta = product.astype(jnp.float32) * (2.0 * math.pi / period)
    return (jnp.cos(theta), jnp.sin(theta))


def apply_rows(matrix, stacked):
    return jnp.einsum("kr,jrcd->jkcd", matrix, stacked, precision=PRECISE)


def apply_cols(matrix, stacked):
    return jnp.einsum("uc,jkcd->jkud", matrix, stacked, precision=PRECISE)


def spectral_products(spec_real, spec_imag):
    value_real, grad_real, filt_real = (spec_real[0], spec_real[1], spec_real[2])
    value_imag, grad_imag, filt_imag = (spec_imag[0], spec_imag[1], spec_imag[2])
    conv_real = value_real * filt_real - value_imag * filt_imag
    conv_imag = value_real * filt_imag + value_imag * filt_real
    back_real = grad_real * filt_real + grad_imag * filt_imag
    back_imag = grad_imag * filt_real - grad_real * filt_imag
    corr_real = grad_real * value_real + grad_imag * value_imag
    corr_imag = grad_imag * value_real - grad_real * value_imag
    return ((conv_real, back_real, corr_real), (conv_imag, back_imag, corr_imag))


def sum_filter(corr_flat):
    return lax.psum_scatter(corr_flat, "dp", scatter_dimension=1, tiled=True)


def spread_rows(stacked, row_devs, col_devs):
    count, rows_here, columns, channels = stacked.shape
    col_block = columns // (row_devs * col_devs)
    pieces = stacked.reshape(count, rows_here, row_devs * col_devs, col_block, channels)
    moved = lax.all_to_all(pieces, ("trow", "tcol"), split_axis=2, concat_axis=1, tiled=True)
    return moved.reshape(count, row_devs * col_devs * rows_here, col_block, channels)


def spread_spectrum(stacked, row_devs, col_devs):
    count, pair, all_rows, col_block, channels = stacked.shape
    row_block = all_rows // (row_devs * col_devs)
    pieces = stacked.reshape(count, pair, row_devs * col_devs, row_block, col_block, channels)
    moved = lax.all_to_all(pieces, ("trow", "tcol"), split_axis=2, concat_axis=4, tiled=True)
    return moved.reshape(count, pair, row_block, row_devs * col_devs * col_block, channels)


def collect_spectrum(stacked, row_devs, col_devs):
    count, pair, row_block, columns, channels = stacked.shape
    col_block = columns // (row_devs * col_devs)
    pieces = stacked.reshape(count, pair, row_block, row_devs * col_devs, col_block, channels)
    moved = lax.all_to_all(pieces, ("trow", "tcol"), split_axis=3, concat_axis=2, tiled=True)
    return moved.reshape(count, pair, row_devs * col_devs * row_block, col_block, channels)


def collect_rows(stacked, row_devs, col_devs):
    count, half_rows, col_block, channels = stacked.shape
    rows_here = half_rows // (row_devs * col_devs)
    pieces = stacked.reshape(count, row_devs * col_devs, rows_here, col_block, channels)
    moved = lax.all_to_all(pieces, ("trow", "tcol"), split_axis=1, concat_axis=3, tiled=True)
    return moved.reshape(count, rows_here, row_devs * col_devs * col_block, channels)


def forward_transform(stacked, place, row_devs, col_devs):
    count, rows_here, columns, channels = stacked.shape
    group_size = row_devs * col_devs
    half_rows = group_size * rows_here
    all_rows = 2 * half_rows
    col_block = columns // group_size
    period = all_rows * columns
    gathered = spread_rows(stacked, row_devs, col_devs)
    cos_rows, sin_rows = angles(count_up(all_rows), count_up(half_rows), all_rows)
    part_real = apply_rows(cos_rows, gathered)
    part_imag = -apply_rows(sin_rows, gathered)
    col_global = place * col_block + count_up(col_block)
    cos_twid, sin_twid = angles(count_up(all_rows), col_global, period)
    cos_twid = cos_twid[None, :, :, None]
    sin_twid = sin_twid[None, :, :, None]
    twid_real = part_real * cos_twid + part_imag * sin_twid
    twid_imag = part_imag * cos_twid - part_real * sin_twid
    spectrum = spread_spectrum(jnp.stack([twid_real, twid_imag], 1), row_devs, col_devs)
    cos_cols, sin_cols = angles(count_up(columns), count_up(columns), columns)
    spec_real = spectrum[:, 0]
    spec_imag = spectrum[:, 1]
    out_real = apply_cols(cos_cols, spec_real) + apply_cols(sin_cols, spec_imag)
    out_imag = apply_cols(cos_cols, spec_imag) - apply_cols(sin_cols, spec_real)
    return (out_real, out_imag)


def inverse_transform(spec_real, spec_imag, place, row_devs, col_devs):
    count, row_block, columns, channels = spec_real.shape
    group_size = row_devs * col_devs
    col_block = columns // group_size
    all_rows = row_block * group_size
    half_rows = all_rows // 2
    period = all_rows * columns
    cos_cols, sin_cols = angles(count_up(columns), count_up(columns), columns)
    pos_real = apply_cols(cos_cols, spec_real) - apply_cols(sin_cols, spec_imag)
    pos_imag = apply_cols(cos_cols, spec_imag) + apply_cols(sin_cols, spec_real)
    gathered = collect_spectrum(jnp.stack([pos_real, pos_imag], 1), row_devs, col_devs)
    real_part = gathered[:, 0]
    imag_part = gathered[:, 1]
    col_global = place * col_block + count_up(col_block)
    cos_twid, sin_twid = angles(count_up(all_rows), col_global, period)
    cos_twid = cos_twid[None, :, :, None]
    sin_twid = sin_twid[None, :, :, None]
    twid_real = real_part * cos_twid - imag_part * sin_twid
    twid_imag = imag_part * cos_twid + real_part * sin_twid
    cos_rows, sin_rows = angles(count_up(half_rows), count_up(all_rows), all_rows)
    result = apply_rows(cos_rows, twid_real) - apply_rows(sin_rows, twid_imag)
    result = result * (1.0 / period)
    return collect_rows(result, row_devs, col_devs)


def local(gate, value, grad_out, filter_raw):
    row_devs = lax.axis_size("trow")
    col_devs = lax.axis_size("tcol")
    seq_devs = lax.axis_size("dp")
    place = lax.axis_index("trow") * col_devs + lax.axis_index("tcol")
    group_size = row_devs * col_devs
    tokens_here = gate.shape[1]
    channels = gate.shape[2]
    columns = CB * group_size
    rows_here = tokens_here // columns
    seq_length = tokens_here * group_size
    scale = seq_length ** (-0.5)
    gate_flat = gate[0].astype(jnp.float32)
    value_flat = value[0].astype(jnp.float32)
    grad_flat = grad_out[0].astype(jnp.float32)
    filt_flat = filter_raw * scale
    grad_conv = grad_flat * gate_flat
    stacked = jnp.stack([value_flat, grad_conv, filt_flat]).reshape(3, rows_here, columns, channels)
    spec_real, spec_imag = forward_transform(stacked, place, row_devs, col_devs)
    prod_real, prod_imag = spectral_products(spec_real, spec_imag)
    conv_real, back_real, corr_real = prod_real
    conv_imag, back_imag, corr_imag = prod_imag
    results = inverse_transform(
        jnp.stack([conv_real, back_real, corr_real]),
        jnp.stack([conv_imag, back_imag, corr_imag]),
        place,
        row_devs,
        col_devs,
    )
    filt_grad = sum_filter(results[2].reshape(tokens_here, channels))
    conv_flat = results[0].reshape(tokens_here, channels)
    value_grad = results[1].reshape(tokens_here, channels)
    grad_gate = (grad_flat * conv_flat).astype(jnp.bfloat16).reshape(1, tokens_here, channels)
    grad_value = value_grad.astype(jnp.bfloat16).reshape(1, tokens_here, channels)
    grad_filter = filt_grad * scale
    return (grad_gate, grad_value, grad_filter)


def solution(mesh):
    return jax.shard_map(
        local,
        mesh=mesh,
        in_specs=(
            P("dp", ("trow", "tcol"), None),
            P("dp", ("trow", "tcol"), None),
            P("dp", ("trow", "tcol"), None),
            P(("trow", "tcol"), None),
        ),
        out_specs=(
            P("dp", ("trow", "tcol"), None),
            P("dp", ("trow", "tcol"), None),
            P(("trow", "tcol"), "dp"),
        ),
        check_vma=False,
    )
```

profile of v0, /device:TPU:1, one launch (start us, length us, event | category | flops | bytes accessed | tf_op | source)
XLA Modules:
  0.0 214.8 jit_solution(9482158865493894437)
XLA Ops:
  7.2 0.9 convert_element_type.71
  8.0 0.9 multiply_bitcast_fusion
  8.9 0.9 convert_multiply_fusion.1
  9.9 1.1 copy.71
  11.0 18.4 %all-to-all-start = ((f32[3,1,128,1,256]{4,3,1,0,2:T(1,128)}), f32[3,1,128,1,256]{4,3,1,0,2:T(1,128)S(1)}, u32[]{:S(2)}, u32[]{:S(2)}) async-start(f32[3,1,128,1,256]{4,3,1,0,2:T(1,128)} %copy.71), calls=%async_computation | async-start | bytes 786432 | tf_op jit(solution)/shard_map/all_to_all | solution.py:52
  29.4 0.0 reduce-scatter.4.cloned.1.call-start
  29.5 0.1 fusion.81
  29.5 17.5 %all-to-all-done = f32[3,1,128,1,256]{4,3,1,0,2:T(1,128)S(1)} async-done(((f32[3,1,128,1,256]{4,3,1,0,2:T(1,128)}), f32[3,1,128,1,256]{4,3,1,0,2:T(1,128)S(1)}, u32[]{:S(2)}, u32[]{:S(2)}) %all-to-all-start) | async-done | bytes 393248 | tf_op jit(solution)/shard_map/all_to_all | solution.py:52
  47.1 1.3 fusion.4
  48.3 1.4 add_bitcast_fusion
  49.7 0.5 stack.40
  50.2 0.5 stack.41
  50.7 0.7 pad_maximum_fusion
  51.4 0.5 copy.89
  52.0 48.7 %all_to_all.48 = f32[3,2,128,2,1,256]{5,3,0,1,4,2:T(2,128)S(1)} all-to-all(f32[3,2,128,2,1,256]{5,3,0,1,4,2:T(2,128)S(1)} %copy.89), channel_id=1, replica_groups=mesh['dp'=4,'trow'=16,'tcol'=8] {'trow','tcol'}, dimensions={2} | all-to-all | bytes 3145728 | tf_op jit(solution)/shard_map/all_to_all | solution.py:60
  100.6 0.9 copy.75
  101.6 1.0 fusion.15
  102.6 1.0 fusion.14
  103.6 1.0 fusion.2
  104.6 1.0 fusion.3
  105.7 0.1 multiply_add_fusion.2
  105.8 0.1 multiply_subtract_fusion.2
  105.9 1.0 fusion.19
  106.9 1.0 fusion.18
  107.9 1.0 fusion.1
  109.0 1.0 fusion
  110.0 0.1 maximum_bitcast_fusion
  110.1 0.9 copy.76
  111.1 48.4 %all_to_all.49 = f32[3,2,2,128,1,256]{5,2,0,1,4,3:T(2,128)S(1)} all-to-all(f32[3,2,2,128,1,256]{5,2,0,1,4,3:T(2,128)S(1)} %copy.76), channel_id=1, replica_groups=mesh['dp'=4,'trow'=16,'tcol'=8] {'trow','tcol'}, dimensions={3} | all-to-all | bytes 3145728 | tf_op jit(solution)/shard_map/all_to_all | solution.py:68
  159.5 0.8 copy.77
  160.3 1.2 fusion.135
  161.5 1.9 fusion.8
  163.4 1.9 fusion.6
  165.3 0.0 copy-start
  165.3 0.5 copy.81
  165.9 23.3 %all_to_all.50 = f32[3,128,1,1,256]{4,3,2,0,1:T(1,128)S(1)} all-to-all(f32[3,128,1,1,256]{4,3,2,0,1:T(1,128)S(1)} %copy.81), channel_id=1, replica_groups=mesh['dp'=4,'trow'=16,'tcol'=8] {'trow','tcol'}, dimensions={1} | all-to-all | bytes 786432 | tf_op jit(solution)/shard_map/all_to_all | solution.py:76
  189.1 0.2 fusion.136
  189.3 0.8 copy.92
  190.1 0.0 reduce-scatter.4.cloned.1.call-update
  190.1 0.1 slice.68
  190.2 0.6 copy.128
  190.8 0.0 copy-done
  190.8 0.6 fusion.28
  191.5 14.9 %reduce-scatter.4.cloned.1.call-done = f32[64,128]{1,0:T(8,128)} async-done(((f32[256,128]{1,0:T(8,128)}), f32[64,128]{1,0:T(8,128)}) %reduce-scatter.4.cloned.1.call-update) | async-done | bytes 32784
  206.4 0.8 copy.91
  207.2 0.7 copy.84
  (2 shorter events, 0.0 us)
Async XLA Ops:
  11.0 36.0 %all-to-all-start = ((f32[3,1,128,1,256]{4,3,1,0,2:T(1,128)}), f32[3,1,128,1,256]{4,3,1,0,2:T(1,128)S(1)}, u32[]{:S(2)}, u32[]{:S(2)}) async-start(f32[3,1,128,1,256]{4,3,1,0,2:T(1,128)} %copy.71), calls=%async_computation | async-start | bytes 786432 | tf_op jit(solution)/shard_map/all_to_all | solution.py:52
  29.4 176.9 %reduce-scatter.4.cloned.1.call-start = ((), (), s32[]{:S(2)}) async-start(), calls=%async_computation.5 | async-start | bytes 163840
  165.3 25.5 %copy-start = (bf16[1,128,256]{2,1,0:T(8,128)(2,1)S(1)}, bf16[1,128,256]{2,1,0:T(8,128)(2,1)}, u32[]{:S(2)}) copy-start(bf16[1,128,256]{2,1,0:T(8,128)(2,1)} %param.6) | copy-start | bytes 196612
Sparse Core Ops, SparseCore 0:
  190.2 16.0 reduce-scatter.3
where the time goes:
time: 217 us; the launch traced here: 215 us
  blocking collectives  120 us (55%)
  waiting for transfers between devices  32.4 us (15%)
  starting transfers between devices  18.5 us (9%)
  matrix products  14.6 us (7%)
  between operations  14.3 us (7%)
  local copies, waits for them, and re-layouts  10.2 us (5%)
  other arithmetic  4.43 us (2%)
    all_to_all x1, blocking collectives, spread_spectrum(): lax.all_to_all(pieces, ('trow', 'tcol'), split_axis=2, concat_axis=4, til...  48.7 us
    all_to_all x1, blocking collectives, collect_spectrum(): lax.all_to_all(pieces, ('trow', 'tcol'), split_axis=3, concat_axis=2, til...  48.4 us
    all_to_all x1, blocking collectives, collect_rows(): lax.all_to_all(pieces, ('trow', 'tcol'), split_axis=1, concat_axis=3, til...  23.3 us
    all_to_all x1, starting transfers between devices, spread_rows(): lax.all_to_all(pieces, ('trow', 'tcol'), split_axis=2, concat_axis=1, til...  18.4 us
    all_to_all x1, waiting for transfers between devices, spread_rows(): lax.all_to_all(pieces, ('trow', 'tcol'), split_axis=2, concat_axis=1, til...  17.5 us
    unnamed x2, waiting for transfers between devices  14.9 us
    dot_general x8, matrix products, apply_cols(): return jnp.einsum('uc,jkcd->jkud', matrix, stacked, precision=PRECISE)  8.16 us
    dot_general x4, matrix products, apply_rows(): return jnp.einsum('kr,jrcd->jkcd', matrix, stacked, precision=PRECISE)  6.46 us
  transfers between devices with their start and end apart: 2, of which 2 were waited for; matrix products, arithmetic and copies ran while one was open for 1% of the time, Pallas kernels for 0%

commit v1 on v0

v1 whole, which is shorter than its diff:
```python
import jax
import jax.numpy as jnp
import ml_dtypes
import numpy as np
from jax import lax
from jax.experimental import pallas as pl
from jax.experimental.pallas import tpu as pltpu
from jax.sharding import PartitionSpec as P

MESH = pl.DeviceIdType.MESH
LANES = 128
F32 = jnp.float32
BF16 = jnp.bfloat16


def row_of(trow, tcol):
    y_lo, z = trow // 8, trow % 8
    return (z % 4) * 32 + (y_lo * 2 + z // 4) * 8 + tcol


def split_const(matrix):
    high = matrix.astype(np.float32).astype(ml_dtypes.bfloat16)
    low = (matrix - high.astype(np.float64)).astype(np.float32).astype(ml_dtypes.bfloat16)
    return high, low


def constants():
    block = np.zeros(LANES, np.int64)
    for trow in range(16):
        for tcol in range(8):
            block[row_of(trow, tcol)] = trow * 8 + tcol
    odd = 2 * np.arange(LANES) + 1
    theta = 2 * np.pi * ((odd[:, None] * block[None, :]) % 512) / 512
    wide = np.zeros((2, 2, LANES, LANES, 2))
    for half in range(2):
        wide[0, half, :, :, half] = np.cos(theta)
        wide[1, half, :, :, half] = -np.sin(theta)
    outer = wide.reshape(4 * LANES, 2 * LANES)
    place = np.arange(LANES)
    angle = 2 * np.pi * ((place[:, None] * place[None, :]) % LANES) / LANES
    cos, sin = np.cos(angle), np.sin(angle)
    inner = np.block([[cos, -sin], [sin, cos]])
    back = np.block([[cos, sin], [-sin, cos]])
    phi = 2 * np.pi * (odd[:, None] * place[None, :]) / 65536
    scale = 2.0 ** -21
    return (
        np.stack(split_const(outer)),
        np.stack(split_const(inner) + split_const(back)),
        np.stack(split_const(outer.T * scale)),
        np.stack([np.cos(phi), np.sin(phi)]).astype(np.float32),
    )


def halves(x):
    high = x.astype(BF16)
    low = (x - high.astype(F32)).astype(BF16)
    return high, low


def dot(a, b):
    return jnp.dot(a, b, preferred_element_type=F32)


def outer_dot(mat_high, mat_low, x):
    high, low = halves(x)
    both = dot(mat_high, jnp.concatenate([high, low], axis=1))
    return both[:, :LANES] + both[:, LANES:] + dot(mat_low, high)


def inner_dot(x, mat_high, mat_low):
    high, low = halves(x)
    return dot(high, mat_high) + dot(low, mat_high) + dot(high, mat_low)


def turn(real, imag, cos, sin):
    shape = (2, LANES, LANES)
    real, imag = real.reshape(shape), imag.reshape(shape)
    out_real = real * cos - imag * sin
    out_imag = imag * cos + real * sin
    return out_real.reshape(2 * LANES, LANES), out_imag.reshape(2 * LANES, LANES)


def kernel(
    value_hbm, gate_hbm, grad_hbm, filt_hbm, outer_hbm, inner_hbm, last_hbm, twid_hbm,
    gate_out, value_out, filt_out,
    value_in, gate_in, grad_in, filt_in, outer, inner, last, twid,
    value_send, filt_send,
    grad_send, value_col, grad_col, filt_col,
    conv_col, back_col, corr_col, conv_row, back_row,
    corr_parts, corr_sum, load_sem, send_sem, recv_sem,
):
    seq = lax.axis_index("dp")
    trow = lax.axis_index("trow")
    tcol = lax.axis_index("tcol")
    me = trow * 8 + tcol
    my_row = row_of(trow, tcol)

    loads = [
        pltpu.make_async_copy(src, dst, load_sem.at[i])
        for i, (src, dst) in enumerate(
            (
                (filt_hbm, filt_in),
                (value_hbm, value_in),
                (grad_hbm, grad_in),
                (gate_hbm, gate_in),
                (outer_hbm, outer),
                (inner_hbm, inner),
                (twid_hbm, twid),
                (last_hbm, last),
            )
        )
    ]
    for load in loads:
        load.start()

    barrier = pltpu.get_barrier_semaphore()

    def greet(k, carry):
        peer = me ^ k
        pl.semaphore_signal(
            barrier, inc=1, device_id=(seq, peer // 8, peer % 8), device_id_type=MESH
        )
        return carry

    lax.fori_loop(1, LANES, greet, 0)
    for k in range(1, 4):
        pl.semaphore_signal(
            barrier, inc=1, device_id=(seq ^ k, trow, tcol), device_id_type=MESH
        )

    def spread(rows, out):
        turned = rows.T
        out[pl.ds(0, LANES, stride=2), :] = turned[:LANES]
        out[pl.ds(1, LANES, stride=2), :] = turned[LANES:]

    loads[0].wait()
    spread(filt_in[...], filt_send)
    loads[1].wait()
    spread(value_in[...].astype(F32), value_send)
    loads[2].wait()
    loads[3].wait()
    spread(grad_in[...].astype(F32) * gate_in[...].astype(F32), grad_send)

    pl.semaphore_wait(barrier, LANES - 1 + 3)

    def pair(ref, row):
        return ref.at[pl.ds(pl.multiple_of(row * 2, 2), 2)]

    def to_columns(src, dst, at):
        def send(k, carry):
            peer = me ^ k
            pltpu.make_async_remote_copy(
                pair(src, peer), pair(dst, my_row), send_sem.at[at], recv_sem.at[at],
                device_id=(seq, peer // 8, peer % 8), device_id_type=MESH,
            ).start()
            return carry

        pltpu.make_async_copy(pair(src, me), pair(dst, my_row), recv_sem.at[at]).start()
        lax.fori_loop(1, LANES, send, 0)

    def to_rows(src, dst, at):
        def send(k, carry):
            peer = me ^ k
            peer_row, peer_col = peer // 8, peer % 8
            pltpu.make_async_remote_copy(
                pair(src, row_of(peer_row, peer_col)), pair(dst, me), send_sem.at[at], recv_sem.at[at],
                device_id=(seq, peer_row, peer_col), device_id_type=MESH,
            ).start()
            return carry

        pltpu.make_async_copy(pair(src, my_row), pair(dst, me), recv_sem.at[at]).start()
        lax.fori_loop(1, LANES, send, 0)

    def take(view, sem):
        pltpu.make_async_copy(view, view, sem).wait()

    quarter = 2 * LANES // 4
    my_turn = trow % 4 == seq

    @pl.when(my_turn)
    def _():
        to_columns(filt_send, filt_col, 0)

    to_columns(value_send, value_col, 1)
    to_columns(grad_send, grad_col, 2)

    def forward(column):
        spec = outer_dot(outer[0], outer[1], column)
        real, imag = turn(spec[: 2 * LANES], spec[2 * LANES :], twid[0], -twid[1])
        spec = inner_dot(jnp.concatenate([real, imag], axis=1), inner[0], inner[1])
        return spec[:, :LANES], spec[:, LANES:]

    def inverse(real, imag):
        spec = inner_dot(jnp.concatenate([real, imag], axis=1), inner[2], inner[3])
        real, imag = turn(spec[:, :LANES], spec[:, LANES:], twid[0], twid[1])
        return outer_dot(last[0], last[1], jnp.concatenate([real, imag], axis=0))

    mine = filt_col.at[pl.ds(pl.multiple_of(seq * quarter, quarter), quarter)]
    take(mine, recv_sem.at[0])
    for k in range(1, 4):
        pltpu.make_async_remote_copy(
            mine, mine, send_sem.at[3], recv_sem.at[3],
            device_id=(seq ^ k, trow, tcol), device_id_type=MESH,
        ).start()

    for load in loads[4:]:
        load.wait()
    take(value_col, recv_sem.at[1])
    value_real, value_imag = forward(value_col[...])
    take(filt_col.at[pl.ds(0, 3 * quarter)], recv_sem.at[3])
    filt_real, filt_imag = forward(filt_col[...])
    conv_col[...] = inverse(
        value_real * filt_real - value_imag * filt_imag,
        value_real * filt_imag + value_imag * filt_real,
    )
    to_rows(conv_col, conv_row, 4)

    take(grad_col, recv_sem.at[2])
    grad_real, grad_imag = forward(grad_col[...])
    corr = inverse(
        grad_real * value_real + grad_imag * value_imag,
        grad_imag * value_real - grad_real * value_imag,
    )
    corr_col[...] = corr
    for half in range(2):
        corr_parts[3 + half] = corr_col[pl.ds(half, LANES, stride=2), :]
    for half in range(2):
        owner = half * 2 + me // 64

        @pl.when(owner != seq)
        def _():
            pltpu.make_async_remote_copy(
                corr_parts.at[3 + half], corr_parts.at[(seq ^ owner) - 1], send_sem.at[6 + half], recv_sem.at[6],
                device_id=(owner, trow, tcol), device_id_type=MESH,
            ).start()

    back_col[...] = inverse(
        grad_real * filt_real + grad_imag * filt_imag,
        grad_imag * filt_real - grad_real * filt_imag,
    )
    to_rows(back_col, back_row, 5)

    own_half = seq // 2
    summing = me // 64 == seq % 2

    @pl.when(summing)
    def _():
        take(corr_parts.at[pl.ds(0, 3)], recv_sem.at[6])
        own = jnp.where(own_half == 0, corr_parts[3], corr_parts[4])
        corr_sum[...] = own + corr_parts[0] + corr_parts[1] + corr_parts[2]
        at = me % 64

        def send(k, carry):
            peer = me ^ k
            peer_row, peer_col = peer // 8, peer % 8
            pltpu.make_async_remote_copy(
                corr_sum.at[pl.ds(row_of(peer_row, peer_col), 1)], filt_out.at[pl.ds(at, 1)],
                send_sem.at[8], recv_sem.at[7],
                device_id=(seq, peer_row, peer_col), device_id_type=MESH,
            ).start()
            return carry

        pltpu.make_async_copy(
            corr_sum.at[pl.ds(my_row, 1)], filt_out.at[pl.ds(at, 1)], recv_sem.at[7]
        ).start()
        lax.fori_loop(1, LANES, send, 0)

    def gather(rows):
        return jnp.concatenate(
            [rows[pl.ds(0, LANES, stride=2), :].T, rows[pl.ds(1, LANES, stride=2), :].T], axis=1
        )

    take(conv_row, recv_sem.at[4])
    gate_out[...] = (grad_in[...].astype(F32) * gather(conv_row)).astype(BF16)
    take(back_row, recv_sem.at[5])
    value_out[...] = gather(back_row).astype(BF16)
    take(filt_out, recv_sem.at[7])

    most = pl.ds(0, 2 * LANES - 2)

    @pl.when(my_turn)
    def _():
        take(filt_send.at[most], send_sem.at[0])

    take(value_send.at[most], send_sem.at[1])
    take(grad_send.at[most], send_sem.at[2])
    take(filt_col.at[pl.ds(0, 3 * quarter)], send_sem.at[3])
    take(conv_col.at[most], send_sem.at[4])
    take(back_col.at[most], send_sem.at[5])
    for half in range(2):
        owner = half * 2 + me // 64

        @pl.when(owner != seq)
        def _():
            take(corr_parts.at[3 + half], send_sem.at[6 + half])

    @pl.when(summing)
    def _():
        take(corr_sum.at[pl.ds(0, LANES - 1)], send_sem.at[8])


def local(gate, value, grad_out, filter_raw):
    wide = pltpu.VMEM((2 * LANES, LANES), F32)
    bf16 = pltpu.VMEM((LANES, 2 * LANES), BF16)
    scratch = [
        bf16, bf16, bf16, pltpu.VMEM((LANES, 2 * LANES), F32),
        pltpu.VMEM((2, 4 * LANES, 2 * LANES), BF16),
        pltpu.VMEM((4, 2 * LANES, 2 * LANES), BF16),
        pltpu.VMEM((2, 2 * LANES, 4 * LANES), BF16),
        pltpu.VMEM((2, LANES, LANES), F32),
    ]
    scratch += [wide] * 11
    scratch += [
        pltpu.VMEM((5, LANES, LANES), F32),
        pltpu.VMEM((LANES, LANES), F32),
        pltpu.SemaphoreType.DMA((8,)),
        pltpu.SemaphoreType.DMA((9,)),
        pltpu.SemaphoreType.DMA((8,)),
    ]
    grad_gate, grad_value, grad_filter = pl.pallas_call(
        kernel,
        name="gated_conv_backward",
        out_shape=(
            jax.ShapeDtypeStruct((LANES, 2 * LANES), BF16),
            jax.ShapeDtypeStruct((LANES, 2 * LANES), BF16),
            jax.ShapeDtypeStruct((LANES // 2, LANES), F32),
        ),
        in_specs=[pl.BlockSpec(memory_space=pl.ANY)] * 8,
        out_specs=(pl.BlockSpec(memory_space=pltpu.VMEM),) * 3,
        scratch_shapes=scratch,
        compiler_params=pltpu.CompilerParams(
            collective_id=0, has_side_effects=True, vmem_limit_bytes=32 << 20
        ),
    )(value[0], gate[0], grad_out[0], filter_raw, *(jnp.asarray(c) for c in constants()))
    return grad_gate[None], grad_value[None], grad_filter.T


def solution(mesh):
    tokens = P("dp", ("trow", "tcol"), None)
    return jax.shard_map(
        local,
        mesh=mesh,
        in_specs=(tokens, tokens, tokens, P(("trow", "tcol"), None)),
        out_specs=(tokens, tokens, P(("trow", "tcol"), "dp")),
        check_vma=False,
    )
```

time: 217 us -> 62.7 us (0.29)
  blocking collectives: 120 us -> 0 us
  Pallas kernels: 0 us -> 52.2 us
  waiting for transfers between devices: 32.4 us -> 0 us
  starting transfers between devices: 18.5 us -> 0 us
  matrix products: 14.6 us -> 0 us
  between operations: 14.3 us -> 0.66 us
  other arithmetic: 4.43 us -> 0 us
    all_to_all x3 -> x0, blocking collectives: 120 us -> none  [the longest x1 48.7 us: spread_spectrum(): lax.all_to_all(pieces, ('trow', 'tcol'), split_axis=2, concat_axis=4, til...]
    pallas_call x0 -> x1, Pallas kernels: none -> 52.2 us  [local(): pl.pallas_call(kernel, name='gated_conv_backward', out_shape=(jax.ShapeDt...]
    all_to_all x1 -> x0, starting transfers between devices: 18.4 us -> none  [spread_rows(): lax.all_to_all(pieces, ('trow', 'tcol'), split_axis=2, concat_axis=1, til...]
    all_to_all x1 -> x0, waiting for transfers between devices: 17.5 us -> none  [spread_rows(): lax.all_to_all(pieces, ('trow', 'tcol'), split_axis=2, concat_axis=1, til...]
    unnamed x2 -> x0, waiting for transfers between devices: 14.9 us -> none
    dot_general x12 -> x0, matrix products: 14.6 us -> none  [the longest x8 8.16 us: apply_cols(): return jnp.einsum('uc,jkcd->jkud', matrix, stacked, precision=PRECISE)]
    unnamed x6 -> x19, local copies, waits for them, and re-layouts: 2.94 us -> 9.32 us
    another operation x4 -> x0, local copies, waits for them, and re-layouts: 2.61 us -> none  [the longest x3 1.47 us: forward_transform(): jnp.stack([twid_real, twid_imag], 1)]
  transfers between devices with their start and end apart: 2 -> 0, of which waited for: 2 -> 0; matrix products, arithmetic and copies ran while one was open for 1% -> 0% of each run, Pallas kernels for 0% -> 0%
where the time goes in v1:
time: 62.7 us; the launch traced here: 62.2 us
  Pallas kernels  52.2 us (83%)
  local copies, waits for them, and re-layouts  9.32 us (15%)
  between operations  0.66 us (1%)
    pallas_call x1, Pallas kernels, local(): pl.pallas_call(kernel, name='gated_conv_backward', out_shape=(jax.ShapeDt...  52.2 us
    unnamed x19, local copies, waits for them, and re-layouts  9.32 us

profile of v1, /device:TPU:1, one launch (start us, length us, event | category | flops | bytes accessed | tf_op | source)
XLA Modules:
  0.0 62.2 jit_solution(12287110956355500073)
XLA Ops:
  0.6 0.0 copy-start
  0.6 1.0 %copy-done = bf16[2,256,512]{2,1,0:T(8,128)(2,1)S(1)} copy-done((bf16[2,256,512]{2,1,0:T(8,128)(2,1)S(1)}, bf16[2,256,512]{2,1,0:T(8,128)(2,1)}, u32[]{:S(2)}) %copy-start) | copy-done | bytes 524312
  1.7 0.0 copy-start.1
  1.7 1.0 %copy-done.1 = bf16[4,256,256]{2,1,0:T(8,128)(2,1)S(1)} copy-done((bf16[4,256,256]{2,1,0:T(8,128)(2,1)S(1)}, bf16[4,256,256]{2,1,0:T(8,128)(2,1)}, u32[]{:S(2)}) %copy-start.1) | copy-done | bytes 524312
  2.7 0.0 copy-start.2
  2.7 1.0 %copy-done.2 = bf16[2,512,256]{2,1,0:T(8,128)(2,1)S(1)} copy-done((bf16[2,512,256]{2,1,0:T(8,128)(2,1)S(1)}, bf16[2,512,256]{2,1,0:T(8,128)(2,1)}, u32[]{:S(2)}) %copy-start.2) | copy-done | bytes 524312
  3.8 0.0 copy-start.3
  3.8 0.9 %copy-done.3 = f32[128,256]{1,0:T(8,128)S(1)} copy-done((f32[128,256]{1,0:T(8,128)S(1)}, f32[128,256]{1,0:T(8,128)}, u32[]{:S(2)}) %copy-start.3) | copy-done | bytes 131096
  4.7 0.0 copy-start.4
  4.7 0.9 %copy-done.4 = f32[2,128,128]{2,1,0:T(8,128)S(1)} copy-done((f32[2,128,128]{2,1,0:T(8,128)S(1)}, f32[2,128,128]{2,1,0:T(8,128)}, u32[]{:S(2)}) %copy-start.4) | copy-done | bytes 131096
  5.6 0.0 copy-start.5
  5.6 0.8 %copy-done.5 = bf16[1,128,256]{2,1,0:T(8,128)(2,1)S(1)} copy-done((bf16[1,128,256]{2,1,0:T(8,128)(2,1)S(1)}, bf16[1,128,256]{2,1,0:T(8,128)(2,1)}, u32[]{:S(2)}) %copy-start.5) | copy-done | bytes 65560
  6.4 0.0 copy-start.6
  6.4 0.8 %copy-done.6 = bf16[1,128,256]{2,1,0:T(8,128)(2,1)S(1)} copy-done((bf16[1,128,256]{2,1,0:T(8,128)(2,1)S(1)}, bf16[1,128,256]{2,1,0:T(8,128)(2,1)}, u32[]{:S(2)}) %copy-start.6) | copy-done | bytes 65560
  7.2 0.0 copy-start.7
  7.3 0.8 %copy-done.7 = bf16[1,128,256]{2,1,0:T(8,128)(2,1)S(1)} copy-done((bf16[1,128,256]{2,1,0:T(8,128)(2,1)S(1)}, bf16[1,128,256]{2,1,0:T(8,128)(2,1)}, u32[]{:S(2)}) %copy-start.7) | copy-done | bytes 65560
  8.1 52.2 %gated_conv_backward.1 = (bf16[128,256]{1,0:T(8,128)(2,1)S(1)}, bf16[128,256]{1,0:T(8,128)(2,1)S(1)}, f32[64,128]{1,0:T(8,128)S(1)}) custom-call(bf16[128,256]{1,0:T(8,128)(2,1)S(1)} %bitcast.6, bf16[128,256]{1,0:T(8,128)(2,1)S(1)} %bitcast.7, bf16[128,256]{1,0:T(8,128)(2,1)S(1)} %bitcast.8, f32[128,256]{1,0:T(8,128)S(1)} %copy-done.3, ...), custom_call_target="tpu_custom_call" | custom-call | tf_op jit(solution)/shard_map/gated_conv_backward/pallas_call | solution.py:320
  60.3 0.6 %copy.14 = bf16[1,128,256]{2,1,0:T(8,128)(2,1)} copy(bf16[1,128,256]{2,1,0:T(8,128)(2,1)S(1)} %bitcast.10) | data formatting | bytes 131072
  60.9 0.6 %copy.15 = bf16[1,128,256]{2,1,0:T(8,128)(2,1)} copy(bf16[1,128,256]{2,1,0:T(8,128)(2,1)S(1)} %bitcast.9) | data formatting | bytes 131072
  61.5 0.6 copy.16
Async XLA Ops:
  0.6 1.0 %copy-start = (bf16[2,256,512]{2,1,0:T(8,128)(2,1)S(1)}, bf16[2,256,512]{2,1,0:T(8,128)(2,1)}, u32[]{:S(2)}) copy-start(bf16[2,256,512]{2,1,0:T(8,128)(2,1)} %constant.10.clone.last_hbm) | copy-start | bytes 1572868
  1.7 1.0 %copy-start.1 = (bf16[4,256,256]{2,1,0:T(8,128)(2,1)S(1)}, bf16[4,256,256]{2,1,0:T(8,128)(2,1)}, u32[]{:S(2)}) copy-start(bf16[4,256,256]{2,1,0:T(8,128)(2,1)} %constant.9.clone.inner_hbm) | copy-start | bytes 1572868
  2.7 1.0 %copy-start.2 = (bf16[2,512,256]{2,1,0:T(8,128)(2,1)S(1)}, bf16[2,512,256]{2,1,0:T(8,128)(2,1)}, u32[]{:S(2)}) copy-start(bf16[2,512,256]{2,1,0:T(8,128)(2,1)} %constant.8.clone.outer_hbm) | copy-start | bytes 1572868
  3.8 0.9 %copy-start.3 = (f32[128,256]{1,0:T(8,128)S(1)}, f32[128,256]{1,0:T(8,128)}, u32[]{:S(2)}) copy-start(f32[128,256]{1,0:T(8,128)} %filt_hbm.1) | copy-start | bytes 393220
  4.7 0.9 %copy-start.4 = (f32[2,128,128]{2,1,0:T(8,128)S(1)}, f32[2,128,128]{2,1,0:T(8,128)}, u32[]{:S(2)}) copy-start(f32[2,128,128]{2,1,0:T(8,128)} %constant.11.clone.twid_hbm) | copy-start | bytes 393220
  5.6 0.8 %copy-start.5 = (bf16[1,128,256]{2,1,0:T(8,128)(2,1)S(1)}, bf16[1,128,256]{2,1,0:T(8,128)(2,1)}, u32[]{:S(2)}) copy-start(bf16[1,128,256]{2,1,0:T(8,128)(2,1)} %param.9) | copy-start | bytes 196612
  6.4 0.8 %copy-start.6 = (bf16[1,128,256]{2,1,0:T(8,128)(2,1)S(1)}, bf16[1,128,256]{2,1,0:T(8,128)(2,1)}, u32[]{:S(2)}) copy-start(bf16[1,128,256]{2,1,0:T(8,128)(2,1)} %param.8) | copy-start | bytes 196612
  7.2 0.8 %copy-start.7 = (bf16[1,128,256]{2,1,0:T(8,128)(2,1)S(1)}, bf16[1,128,256]{2,1,0:T(8,128)(2,1)}, u32[]{:S(2)}) copy-start(bf16[1,128,256]{2,1,0:T(8,128)(2,1)} %param.10) | copy-start | bytes 196612

commit v2 on v1

--- a/solution.py
+++ b/solution.py
@@ -1,3 +1,5 @@
+import functools
+
 import jax
 import jax.numpy as jnp
 import ml_dtypes
@@ -14,8 +16,7 @@
 
 
 def row_of(trow, tcol):
-    y_lo, z = trow // 8, trow % 8
-    return (z % 4) * 32 + (y_lo * 2 + z // 4) * 8 + tcol
+    return ((trow & 3) << 5) | ((trow >> 2) << 3) | tcol
 
 
 def split_const(matrix):
@@ -51,6 +52,45 @@
     )
 
 
+def each_peer(trow, tcol, act):
+    y, z, core = (tcol & 6) | (trow >> 3), trow & 7, tcol & 1
+
+    def column(dz, own):
+        peer_z = (z + dz) & 7
+        for dy in (4, 3, 5, 2, 6, 1, 7, 0):
+            peer_y = (y + dy) & 7
+            peer_row, peer_col = ((peer_y & 1) << 3) | peer_z, (peer_y & 6) | core
+            act(peer_row, peer_col ^ 1)
+            if not (own and dy == 0):
+                act(peer_row, peer_col)
+
+    def step(t, carry):
+        away = (t + 1) >> 1
+        column(jnp.where((t & 1) == 1, 4 - away, 4 + away), False)
+        return carry
+
+    lax.fori_loop(0, 7, step, 0)
+    column(0, True)
+
+
+def each_peer_late(trow, tcol, act):
+    y, z, core = (tcol & 6) | (trow >> 3), trow & 7, tcol & 1
+
+    def step(t, carry):
+        peer_z = ((z + 1 + t) & 3) | ((~t) & 4)
+        for dy in (4, 3, 5, 2, 6, 1, 7, 0):
+            peer_y = (y + dy) & 7
+            peer_row, peer_col = ((peer_y & 1) << 3) | peer_z, (peer_y & 6) | core
+            act(peer_row, peer_col ^ 1)
+            if dy:
+                act(peer_row, peer_col)
+            else:
+                pl.when(peer_z != z)(functools.partial(act, peer_row, peer_col))
+        return carry
+
+    lax.fori_loop(0, 8, step, 0)
+
+
 def halves(x):
     high = x.astype(BF16)
     low = (x - high.astype(F32)).astype(BF16)
@@ -94,6 +134,19 @@
     tcol = lax.axis_index("tcol")
     me = trow * 8 + tcol
     my_row = row_of(trow, tcol)
+
+    barrier = pltpu.get_barrier_semaphore()
+
+    def greet(peer_row, peer_col):
+        pl.semaphore_signal(
+            barrier, inc=1, device_id=(seq, peer_row, peer_col), device_id_type=MESH
+        )
+
+    each_peer(trow, tcol, greet)
+    for k in range(1, 4):
+        pl.semaphore_signal(
+            barrier, inc=1, device_id=(seq ^ k, trow, tcol), device_id_type=MESH
+        )
 
     loads = [
         pltpu.make_async_copy(src, dst, load_sem.at[i])
@@ -113,21 +166,6 @@
     for load in loads:
         load.start()
 
-    barrier = pltpu.get_barrier_semaphore()
-
-    def greet(k, carry):
-        peer = me ^ k
-        pl.semaphore_signal(
-            barrier, inc=1, device_id=(seq, peer // 8, peer % 8), device_id_type=MESH
-        )
-        return carry
-
-    lax.fori_loop(1, LANES, greet, 0)
-    for k in range(1, 4):
-        pl.semaphore_signal(
-            barrier, inc=1, device_id=(seq ^ k, trow, tcol), device_id_type=MESH
-        )
-
     def spread(rows, out):
         turned = rows.T
         out[pl.ds(0, LANES, stride=2), :] = turned[:LANES]
@@ -147,39 +185,55 @@
         return ref.at[pl.ds(pl.multiple_of(row * 2, 2), 2)]
 
     def to_columns(src, dst, at):
-        def send(k, carry):
-            peer = me ^ k
+        there = pair(dst, my_row)
+
+        def send(peer_row, peer_col):
             pltpu.make_async_remote_copy(
-                pair(src, peer), pair(dst, my_row), send_sem.at[at], recv_sem.at[at],
-                device_id=(seq, peer // 8, peer % 8), device_id_type=MESH,
-            ).start()
-            return carry
-
-        pltpu.make_async_copy(pair(src, me), pair(dst, my_row), recv_sem.at[at]).start()
-        lax.fori_loop(1, LANES, send, 0)
-
-    def to_rows(src, dst, at):
-        def send(k, carry):
-            peer = me ^ k
-            peer_row, peer_col = peer // 8, peer % 8
-            pltpu.make_async_remote_copy(
-                pair(src, row_of(peer_row, peer_col)), pair(dst, me), send_sem.at[at], recv_sem.at[at],
+                pair(src, peer_row * 8 + peer_col), there, send_sem.at[at], recv_sem.at[at],
                 device_id=(seq, peer_row, peer_col), device_id_type=MESH,
             ).start()
-            return carry
-
-        pltpu.make_async_copy(pair(src, my_row), pair(dst, me), recv_sem.at[at]).start()
-        lax.fori_loop(1, LANES, send, 0)
+
+        pltpu.make_async_copy(pair(src, me), there, recv_sem.at[at]).start()
+        each_peer_late(trow, tcol, send)
+
+    def to_rows(src, dst, at):
+        there = pair(dst, me)
+
+        def send(peer_row, peer_col):
+            pltpu.make_async_remote_copy(
+                pair(src, row_of(peer_row, peer_col)), there, send_sem.at[at], recv_sem.at[at],
+                device_id=(seq, peer_row, peer_col), device_id_type=MESH,
+            ).start()
+
+        pltpu.make_async_copy(pair(src, my_row), there, recv_sem.at[at]).start()
+        each_peer(trow, tcol, send)
 
     def take(view, sem):
         pltpu.make_async_copy(view, view, sem).wait()
 
     quarter = 2 * LANES // 4
-    my_turn = trow % 4 == seq
-
-    @pl.when(my_turn)
+
+    filt_there = pair(filt_col, my_row)
+
+    def send_filt(peer_row, peer_col):
+        pltpu.make_async_remote_copy(
+            pair(filt_send, peer_row * 8 + peer_col), filt_there, send_sem.at[0], recv_sem.at[0],
+            device_id=(seq, peer_row, peer_col), device_id_type=MESH,
+        ).start()
+
+    for high in (4, 0):
+        peer_z = ((trow ^ seq) & 3) | high
+        for y_lo in (8, 0):
+            for j in range(7, -1, -1):
+                peer_row, peer_col = ((trow & 8) ^ y_lo) | peer_z, tcol ^ j
+                if y_lo or j:
+                    send_filt(peer_row, peer_col)
+                else:
+                    pl.when(peer_row != trow)(functools.partial(send_filt, peer_row, peer_col))
+
+    @pl.when(seq == 0)
     def _():
-        to_columns(filt_send, filt_col, 0)
+        pltpu.make_async_copy(pair(filt_send, me), filt_there, recv_sem.at[0]).start()
 
     to_columns(value_send, value_col, 1)
     to_columns(grad_send, grad_col, 2)
@@ -195,7 +249,7 @@
         real, imag = turn(spec[:, :LANES], spec[:, LANES:], twid[0], twid[1])
         return outer_dot(last[0], last[1], jnp.concatenate([real, imag], axis=0))
 
-    mine = filt_col.at[pl.ds(pl.multiple_of(seq * quarter, quarter), quarter)]
+    mine = filt_col.at[pl.ds(pl.multiple_of((seq ^ (trow & 3)) * quarter, quarter), quarter)]
     take(mine, recv_sem.at[0])
     for k in range(1, 4):
         pltpu.make_async_remote_copy(
@@ -225,7 +279,7 @@
     for half in range(2):
         corr_parts[3 + half] = corr_col[pl.ds(half, LANES, stride=2), :]
     for half in range(2):
-        owner = half * 2 + me // 64
+        owner = half * 2 + (me >> 6)
 
         @pl.when(owner != seq)
         def _():
@@ -240,30 +294,27 @@
     )
     to_rows(back_col, back_row, 5)
 
-    own_half = seq // 2
-    summing = me // 64 == seq % 2
+    own_half = seq >> 1
+    summing = (me >> 6) == (seq & 1)
 
     @pl.when(summing)
     def _():
         take(corr_parts.at[pl.ds(0, 3)], recv_sem.at[6])
         own = jnp.where(own_half == 0, corr_parts[3], corr_parts[4])
         corr_sum[...] = own + corr_parts[0] + corr_parts[1] + corr_parts[2]
-        at = me % 64
-
-        def send(k, carry):
-            peer = me ^ k
-            peer_row, peer_col = peer // 8, peer % 8
+        at = me & 63
+
+        def send(peer_row, peer_col):
             pltpu.make_async_remote_copy(
                 corr_sum.at[pl.ds(row_of(peer_row, peer_col), 1)], filt_out.at[pl.ds(at, 1)],
                 send_sem.at[8], recv_sem.at[7],
                 device_id=(seq, peer_row, peer_col), device_id_type=MESH,
             ).start()
-            return carry
 
         pltpu.make_async_copy(
             corr_sum.at[pl.ds(my_row, 1)], filt_out.at[pl.ds(at, 1)], recv_sem.at[7]
         ).start()
-        lax.fori_loop(1, LANES, send, 0)
+        each_peer(trow, tcol, send)
 
     def gather(rows):
         return jnp.concatenate(
@@ -278,9 +329,13 @@
 
     most = pl.ds(0, 2 * LANES - 2)
 
-    @pl.when(my_turn)
+    @pl.when(seq == 0)
     def _():
-        take(filt_send.at[most], send_sem.at[0])
+        take(filt_send.at[pl.ds(0, quarter - 2)], send_sem.at[0])
+
+    @pl.when(seq != 0)
+    def _():
+        take(filt_send.at[pl.ds(0, quarter)], send_sem.at[0])
 
     take(value_send.at[most], send_sem.at[1])
     take(grad_send.at[most], send_sem.at[2])
@@ -288,7 +343,7 @@
     take(conv_col.at[most], send_sem.at[4])
     take(back_col.at[most], send_sem.at[5])
     for half in range(2):
-        owner = half * 2 + me // 64
+        owner = half * 2 + (me >> 6)
 
         @pl.when(owner != seq)
         def _():
@@ -297,6 +352,17 @@
     @pl.when(summing)
     def _():
         take(corr_sum.at[pl.ds(0, LANES - 1)], send_sem.at[8])
+
+
+def store(gate_in, value_in, filt_in, gate_out, value_out, filt_out, sem):
+    copies = [
+        pltpu.make_async_copy(src, dst, sem.at[i])
+        for i, (src, dst) in enumerate(((gate_in, gate_out), (value_in, value_out), (filt_in, filt_out)))
+    ]
+    for copy in copies:
+        copy.start()
+    for copy in copies:
+        copy.wait()
 
 
 def local(gate, value, grad_out, filter_raw):
@@ -317,21 +383,30 @@
         pltpu.SemaphoreType.DMA((9,)),
         pltpu.SemaphoreType.DMA((8,)),
     ]
-    grad_gate, grad_value, grad_filter = pl.pallas_call(
+    shapes = (
+        jax.ShapeDtypeStruct((LANES, 2 * LANES), BF16),
+        jax.ShapeDtypeStruct((LANES, 2 * LANES), BF16),
+        jax.ShapeDtypeStruct((LANES // 2, LANES), F32),
+    )
+    results = pl.pallas_call(
         kernel,
         name="gated_conv_backward",
-        out_shape=(
-            jax.ShapeDtypeStruct((LANES, 2 * LANES), BF16),
-            jax.ShapeDtypeStruct((LANES, 2 * LANES), BF16),
-            jax.ShapeDtypeStruct((LANES // 2, LANES), F32),
-        ),
-        in_specs=[pl.BlockSpec(memory_space=pl.ANY)] * 8,
+        out_shape=shapes,
+        in_specs=[pl.BlockSpec(memory_space=pltpu.HBM)] * 8,
         out_specs=(pl.BlockSpec(memory_space=pltpu.VMEM),) * 3,
         scratch_shapes=scratch,
         compiler_params=pltpu.CompilerParams(
             collective_id=0, has_side_effects=True, vmem_limit_bytes=32 << 20
         ),
-    )(value[0], gate[0], grad_out[0], filter_raw, *(jnp.asarray(c) for c in constants()))
+    )(*(pltpu.with_memory_space_constraint(x, pltpu.HBM) for x in (value[0], gate[0], grad_out[0], filter_raw, *(jnp.asarray(c) for c in constants()))))
+    grad_gate, grad_value, grad_filter = pl.pallas_call(
+        store,
+        name="store_results",
+        out_shape=shapes,
+        in_specs=[pl.BlockSpec(memory_space=pltpu.VMEM)] * 3,
+        out_specs=(pl.BlockSpec(memory_space=pltpu.HBM),) * 3,
+        scratch_shapes=[pltpu.SemaphoreType.DMA((3,))],
+    )(*(pltpu.with_memory_space_constraint(r, pltpu.VMEM) for r in results))
     return grad_gate[None], grad_value[None], grad_filter.T
 
 

time: 62.7 us -> 44.5 us (0.71)
  local copies, waits for them, and re-layouts: 9.32 us -> 0 us
  Pallas kernels: 52.2 us -> 43.8 us
    unnamed x19 -> x0, local copies, waits for them, and re-layouts: 9.32 us -> none
    pallas_call x1 -> x2, Pallas kernels: 52.2 us -> 43.8 us  [the longest x1 43.1 us: local(): pl.pallas_call(kernel, name='gated_conv_backward', out_shape=shapes, in_s...]
where the time goes in v2:
time: 44.5 us; the launch traced here: 44.4 us
  Pallas kernels  43.8 us (98%)
  between operations  0.64 us (1%)
    pallas_call x1, Pallas kernels, local(): pl.pallas_call(kernel, name='gated_conv_backward', out_shape=shapes, in_s...  43.1 us

profile of v2, /device:TPU:1, one launch (start us, length us, event | category | flops | bytes accessed | tf_op | source)
XLA Modules:
  0.0 44.4 jit_solution(9623148641042861972)
XLA Ops:
  0.6 43.1 %gated_conv_backward.1 = (bf16[128,256]{1,0:T(8,128)(2,1)S(1)}, bf16[128,256]{1,0:T(8,128)(2,1)S(1)}, f32[64,128]{1,0:T(8,128)S(1)}) custom-call(bf16[128,256]{1,0:T(8,128)(2,1)} %bitcast.6, bf16[128,256]{1,0:T(8,128)(2,1)} %bitcast.7, bf16[128,256]{1,0:T(8,128)(2,1)} %bitcast.8, f32[128,256]{1,0:T(8,128)} %filt_hbm.1, ...), custom_call_target="tpu_custom_call" | custom-call | tf_op jit(solution)/shard_map/gated_conv_backward/pallas_call | solution.py:391
  43.7 0.7 %store_results.1 = (bf16[128,256]{1,0:T(8,128)(2,1)}, bf16[128,256]{1,0:T(8,128)(2,1)}, f32[64,128]{1,0:T(8,128)}) custom-call(bf16[128,256]{1,0:T(8,128)(2,1)S(1)} %get-tuple-element.9.gate_in, bf16[128,256]{1,0:T(8,128)(2,1)S(1)} %get-tuple-element.10.value_in, f32[64,128]{1,0:T(8,128)S(1)} %get-tuple-element.11.filt_in), custom_call_target="tpu_custom_call" | custom-call | tf_op jit(solution)/shard_map/store_results/pallas_call | solution.py:402

commit v3 on v2

--- a/solution.py
+++ b/solution.py
@@ -16,7 +16,7 @@
 
 
 def row_of(trow, tcol):
-    return ((trow & 3) << 5) | ((trow >> 2) << 3) | tcol
+    return ((trow & 7) << 4) | ((trow >> 3) << 3) | tcol
 
 
 def split_const(matrix):
@@ -52,32 +52,37 @@
     )
 
 
+def peers_at(trow, tcol, dz, act, skip_me=False):
+    y, z, core = (tcol & 6) | (trow >> 3), trow & 7, tcol & 1
+    for dy in (4, 3, 5, 2, 6, 1, 7, 0):
+        peer_y = (y + dy) & 7
+        peer_row, peer_col = ((peer_y & 1) << 3) | ((z + dz) & 7), (peer_y & 6) | core
+        act(peer_row, peer_col ^ 1)
+        if dy or not skip_me:
+            act(peer_row, peer_col)
+
+
+def far_z(t):
+    away = (t + 1) >> 1
+    return jnp.where((t & 1) == 1, 4 - away, 4 + away)
+
+
 def each_peer(trow, tcol, act):
+    def step(t, carry):
+        peers_at(trow, tcol, far_z(t), act)
+        return carry
+
+    lax.fori_loop(0, 7, step, 0)
+    peers_at(trow, tcol, 0, act, True)
+
+
+CUT = 2
+
+
+def each_of_z(trow, tcol, part, act):
     y, z, core = (tcol & 6) | (trow >> 3), trow & 7, tcol & 1
 
-    def column(dz, own):
-        peer_z = (z + dz) & 7
-        for dy in (4, 3, 5, 2, 6, 1, 7, 0):
-            peer_y = (y + dy) & 7
-            peer_row, peer_col = ((peer_y & 1) << 3) | peer_z, (peer_y & 6) | core
-            act(peer_row, peer_col ^ 1)
-            if not (own and dy == 0):
-                act(peer_row, peer_col)
-
-    def step(t, carry):
-        away = (t + 1) >> 1
-        column(jnp.where((t & 1) == 1, 4 - away, 4 + away), False)
-        return carry
-
-    lax.fori_loop(0, 7, step, 0)
-    column(0, True)
-
-
-def each_peer_late(trow, tcol, act):
-    y, z, core = (tcol & 6) | (trow >> 3), trow & 7, tcol & 1
-
-    def step(t, carry):
-        peer_z = ((z + 1 + t) & 3) | ((~t) & 4)
+    def step(peer_z, carry):
         for dy in (4, 3, 5, 2, 6, 1, 7, 0):
             peer_y = (y + dy) & 7
             peer_row, peer_col = ((peer_y & 1) << 3) | peer_z, (peer_y & 6) | core
@@ -88,7 +93,7 @@
                 pl.when(peer_z != z)(functools.partial(act, peer_row, peer_col))
         return carry
 
-    lax.fori_loop(0, 8, step, 0)
+    lax.fori_loop((0, CUT)[part], (CUT, 8)[part], step, 0)
 
 
 def halves(x):
@@ -127,7 +132,7 @@
     value_send, filt_send,
     grad_send, value_col, grad_col, filt_col,
     conv_col, back_col, corr_col, conv_row, back_row,
-    corr_parts, corr_sum, load_sem, send_sem, recv_sem,
+    corr_parts, corr_sum, load_sem, send_sem, recv_sem, filt_sem,
 ):
     seq = lax.axis_index("dp")
     trow = lax.axis_index("trow")
@@ -168,8 +173,9 @@
 
     def spread(rows, out):
         turned = rows.T
-        out[pl.ds(0, LANES, stride=2), :] = turned[:LANES]
-        out[pl.ds(1, LANES, stride=2), :] = turned[LANES:]
+        for q in range(4):
+            half, core = q // 2, 1 - q % 2
+            out[pl.ds(2 * core + half, LANES // 2, stride=4), :] = turned[64 * q : 64 * q + 64]
 
     loads[0].wait()
     spread(filt_in[...], filt_send)
@@ -194,9 +200,9 @@
             ).start()
 
         pltpu.make_async_copy(pair(src, me), there, recv_sem.at[at]).start()
-        each_peer_late(trow, tcol, send)
-
-    def to_rows(src, dst, at):
+        each_peer(trow, tcol, send)
+
+    def to_rows(src, dst, at, part):
         there = pair(dst, me)
 
         def send(peer_row, peer_col):
@@ -205,8 +211,9 @@
                 device_id=(seq, peer_row, peer_col), device_id_type=MESH,
             ).start()
 
-        pltpu.make_async_copy(pair(src, my_row), there, recv_sem.at[at]).start()
-        each_peer(trow, tcol, send)
+        if part:
+            pltpu.make_async_copy(pair(src, my_row), there, recv_sem.at[at]).start()
+        each_of_z(trow, tcol, part, send)
 
     def take(view, sem):
         pltpu.make_async_copy(view, view, sem).wait()
@@ -217,7 +224,7 @@
 
     def send_filt(peer_row, peer_col):
         pltpu.make_async_remote_copy(
-            pair(filt_send, peer_row * 8 + peer_col), filt_there, send_sem.at[0], recv_sem.at[0],
+            pair(filt_send, peer_row * 8 + peer_col), filt_there, send_sem.at[0], filt_sem.at[trow >> 2 & 1],
             device_id=(seq, peer_row, peer_col), device_id_type=MESH,
         ).start()
 
@@ -233,7 +240,7 @@
 
     @pl.when(seq == 0)
     def _():
-        pltpu.make_async_copy(pair(filt_send, me), filt_there, recv_sem.at[0]).start()
+        pltpu.make_async_copy(pair(filt_send, me), filt_there, filt_sem.at[trow >> 2 & 1]).start()
 
     to_columns(value_send, value_col, 1)
     to_columns(grad_send, grad_col, 2)
@@ -249,83 +256,93 @@
         real, imag = turn(spec[:, :LANES], spec[:, LANES:], twid[0], twid[1])
         return outer_dot(last[0], last[1], jnp.concatenate([real, imag], axis=0))
 
-    mine = filt_col.at[pl.ds(pl.multiple_of((seq ^ (trow & 3)) * quarter, quarter), quarter)]
-    take(mine, recv_sem.at[0])
-    for k in range(1, 4):
-        pltpu.make_async_remote_copy(
-            mine, mine, send_sem.at[3], recv_sem.at[3],
-            device_id=(seq ^ k, trow, tcol), device_id_type=MESH,
-        ).start()
+    for flip in range(2):
+        high = (trow >> 2 & 1) ^ flip
+        take(filt_col.at[pl.ds(0, 32)], filt_sem.at[high])
+        block = filt_col.at[pl.ds(pl.multiple_of((((trow ^ seq) & 3) | (high << 2)) * 32, 32), 32)]
+        for k in (2, 1, 3):
+            pltpu.make_async_remote_copy(
+                block, block, send_sem.at[3], recv_sem.at[3],
+                device_id=(seq ^ k, trow, tcol), device_id_type=MESH,
+            ).start()
 
     for load in loads[4:]:
         load.wait()
     take(value_col, recv_sem.at[1])
     value_real, value_imag = forward(value_col[...])
+    take(grad_col, recv_sem.at[2])
+    grad_real, grad_imag = forward(grad_col[...])
+    corr_col[...] = inverse(
+        grad_real * value_real + grad_imag * value_imag,
+        grad_imag * value_real - grad_real * value_imag,
+    )
+    core = tcol & 1
+    for half in range(2):
+        corr_parts[3 + half] = corr_col[pl.ds(half, LANES, stride=2), :]
+    owners = [half * 2 + 1 - core for half in range(2)]
+    blocks = (pl.ds(0, 16 * CUT), pl.ds(16 * CUT, LANES - 16 * CUT))
+    for part, at in enumerate(blocks):
+        for half, owner in enumerate(owners):
+
+            @pl.when(owner != seq)
+            def _():
+                pltpu.make_async_remote_copy(
+                    corr_parts.at[3 + half, at], corr_parts.at[(seq ^ owner) - 1, at],
+                    send_sem.at[6 + half], recv_sem.at[6 + part],
+                    device_id=(owner, trow, tcol), device_id_type=MESH,
+                ).start()
+
     take(filt_col.at[pl.ds(0, 3 * quarter)], recv_sem.at[3])
     filt_real, filt_imag = forward(filt_col[...])
     conv_col[...] = inverse(
         value_real * filt_real - value_imag * filt_imag,
         value_real * filt_imag + value_imag * filt_real,
     )
-    to_rows(conv_col, conv_row, 4)
-
-    take(grad_col, recv_sem.at[2])
-    grad_real, grad_imag = forward(grad_col[...])
-    corr = inverse(
-        grad_real * value_real + grad_imag * value_imag,
-        grad_imag * value_real - grad_real * value_imag,
-    )
-    corr_col[...] = corr
-    for half in range(2):
-        corr_parts[3 + half] = corr_col[pl.ds(half, LANES, stride=2), :]
-    for half in range(2):
-        owner = half * 2 + (me >> 6)
-
-        @pl.when(owner != seq)
-        def _():
-            pltpu.make_async_remote_copy(
-                corr_parts.at[3 + half], corr_parts.at[(seq ^ owner) - 1], send_sem.at[6 + half], recv_sem.at[6],
-                device_id=(owner, trow, tcol), device_id_type=MESH,
-            ).start()
-
+    to_rows(conv_col, conv_row, 4, 0)
     back_col[...] = inverse(
         grad_real * filt_real + grad_imag * filt_imag,
         grad_imag * filt_real - grad_real * filt_imag,
     )
-    to_rows(back_col, back_row, 5)
-
-    own_half = seq >> 1
-    summing = (me >> 6) == (seq & 1)
+    to_rows(back_col, back_row, 5, 0)
+
+    own = 3 + (seq >> 1)
+    summing = core != (seq & 1)
+    filt_row = filt_out.at[pl.ds(me >> 1, 1)]
+
+    def send_sum(peer_row, peer_col):
+        pltpu.make_async_remote_copy(
+            corr_sum.at[pl.ds(row_of(peer_row, peer_col), 1)], filt_row, send_sem.at[8], recv_sem.at[8],
+            device_id=(seq, peer_row, peer_col), device_id_type=MESH,
+        ).start()
+
+    def send_sums(part):
+        at = blocks[part]
+        take(corr_parts.at[pl.ds(0, 3), at], recv_sem.at[6 + part])
+        corr_sum[at] = corr_parts[own, at] + corr_parts[0, at] + corr_parts[1, at] + corr_parts[2, at]
+        each_of_z(trow, tcol, part, send_sum)
 
     @pl.when(summing)
     def _():
-        take(corr_parts.at[pl.ds(0, 3)], recv_sem.at[6])
-        own = jnp.where(own_half == 0, corr_parts[3], corr_parts[4])
-        corr_sum[...] = own + corr_parts[0] + corr_parts[1] + corr_parts[2]
-        at = me & 63
-
-        def send(peer_row, peer_col):
-            pltpu.make_async_remote_copy(
-                corr_sum.at[pl.ds(row_of(peer_row, peer_col), 1)], filt_out.at[pl.ds(at, 1)],
-                send_sem.at[8], recv_sem.at[7],
-                device_id=(seq, peer_row, peer_col), device_id_type=MESH,
-            ).start()
-
-        pltpu.make_async_copy(
-            corr_sum.at[pl.ds(my_row, 1)], filt_out.at[pl.ds(at, 1)], recv_sem.at[7]
-        ).start()
-        each_peer(trow, tcol, send)
+        send_sums(0)
+
+    to_rows(conv_col, conv_row, 4, 1)
+    to_rows(back_col, back_row, 5, 1)
+
+    @pl.when(summing)
+    def _():
+        send_sums(1)
+        pltpu.make_async_copy(corr_sum.at[pl.ds(my_row, 1)], filt_row, recv_sem.at[8]).start()
 
     def gather(rows):
         return jnp.concatenate(
-            [rows[pl.ds(0, LANES, stride=2), :].T, rows[pl.ds(1, LANES, stride=2), :].T], axis=1
-        )
+            [rows[pl.ds(2 * (1 - q % 2) + q // 2, LANES // 2, stride=4), :] for q in range(4)], axis=0
+        ).T
 
     take(conv_row, recv_sem.at[4])
     gate_out[...] = (grad_in[...].astype(F32) * gather(conv_row)).astype(BF16)
     take(back_row, recv_sem.at[5])
     value_out[...] = gather(back_row).astype(BF16)
-    take(filt_out, recv_sem.at[7])
+    take(filt_out, recv_sem.at[8])
 
     most = pl.ds(0, 2 * LANES - 2)
 
@@ -342,8 +359,7 @@
     take(filt_col.at[pl.ds(0, 3 * quarter)], send_sem.at[3])
     take(conv_col.at[most], send_sem.at[4])
     take(back_col.at[most], send_sem.at[5])
-    for half in range(2):
-        owner = half * 2 + (me >> 6)
+    for half, owner in enumerate(owners):
 
         @pl.when(owner != seq)
         def _():
@@ -381,7 +397,8 @@
         pltpu.VMEM((LANES, LANES), F32),
         pltpu.SemaphoreType.DMA((8,)),
         pltpu.SemaphoreType.DMA((9,)),
-        pltpu.SemaphoreType.DMA((8,)),
+        pltpu.SemaphoreType.DMA((9,)),
+        pltpu.SemaphoreType.DMA((2,)),
     ]
     shapes = (
         jax.ShapeDtypeStruct((LANES, 2 * LANES), BF16),

time: 44.5 us -> 41.1 us (0.924)
  Pallas kernels: 43.8 us -> 40.1 us
    pallas_call x1, Pallas kernels: 43.1 us -> 39.4 us  [local(): pl.pallas_call(kernel, name='gated_conv_backward', out_shape=shapes, in_s...]
where the time goes in v3:
time: 41.1 us; the launch traced here: 40.7 us
  Pallas kernels  40.1 us (98%)
  between operations  0.64 us (2%)
    pallas_call x1, Pallas kernels, local(): pl.pallas_call(kernel, name='gated_conv_backward', out_shape=shapes, in_s...  39.4 us

profile of v3, /device:TPU:1, one launch (start us, length us, event | category | flops | bytes accessed | tf_op | source)
XLA Modules:
  0.0 40.7 jit_solution(10772471255279073730)
XLA Ops:
  0.6 39.4 %gated_conv_backward.1 = (bf16[128,256]{1,0:T(8,128)(2,1)S(1)}, bf16[128,256]{1,0:T(8,128)(2,1)S(1)}, f32[64,128]{1,0:T(8,128)S(1)}) custom-call(bf16[128,256]{1,0:T(8,128)(2,1)} %bitcast.6, bf16[128,256]{1,0:T(8,128)(2,1)} %bitcast.7, bf16[128,256]{1,0:T(8,128)(2,1)} %bitcast.8, f32[128,256]{1,0:T(8,128)} %filt_hbm.1, ...), custom_call_target="tpu_custom_call" | custom-call | tf_op jit(solution)/shard_map/gated_conv_backward/pallas_call | solution.py:408
  40.0 0.7 %store_results.1 = (bf16[128,256]{1,0:T(8,128)(2,1)}, bf16[128,256]{1,0:T(8,128)(2,1)}, f32[64,128]{1,0:T(8,128)}) custom-call(bf16[128,256]{1,0:T(8,128)(2,1)S(1)} %get-tuple-element.9.gate_in, bf16[128,256]{1,0:T(8,128)(2,1)S(1)} %get-tuple-element.10.value_in, f32[64,128]{1,0:T(8,128)S(1)} %get-tuple-element.11.filt_in), custom_call_target="tpu_custom_call" | custom-call | tf_op jit(solution)/shard_map/store_results/pallas_call | solution.py:419

commit v4 on v3

--- a/solution.py
+++ b/solution.py
@@ -32,10 +32,10 @@
             block[row_of(trow, tcol)] = trow * 8 + tcol
     odd = 2 * np.arange(LANES) + 1
     theta = 2 * np.pi * ((odd[:, None] * block[None, :]) % 512) / 512
-    wide = np.zeros((2, 2, LANES, LANES, 2))
+    wide = np.zeros((2, 2, LANES, 2, LANES))
     for half in range(2):
-        wide[0, half, :, :, half] = np.cos(theta)
-        wide[1, half, :, :, half] = -np.sin(theta)
+        wide[0, half, :, half] = np.cos(theta)
+        wide[1, half, :, half] = -np.sin(theta)
     outer = wide.reshape(4 * LANES, 2 * LANES)
     place = np.arange(LANES)
     angle = 2 * np.pi * ((place[:, None] * place[None, :]) % LANES) / LANES
@@ -129,9 +129,8 @@
     value_hbm, gate_hbm, grad_hbm, filt_hbm, outer_hbm, inner_hbm, last_hbm, twid_hbm,
     gate_out, value_out, filt_out,
     value_in, gate_in, grad_in, filt_in, outer, inner, last, twid,
-    value_send, filt_send,
-    grad_send, value_col, grad_col, filt_col,
-    conv_col, back_col, corr_col, conv_row, back_row,
+    both_send, filt_send, both_col, filt_col,
+    conv_col, back_col, conv_row, back_row,
     corr_parts, corr_sum, load_sem, send_sem, recv_sem, filt_sem,
 ):
     seq = lax.axis_index("dp")
@@ -171,35 +170,41 @@
     for load in loads:
         load.start()
 
-    def spread(rows, out):
+    def spread(rows, out, first, count):
         turned = rows.T
         for q in range(4):
             half, core = q // 2, 1 - q % 2
-            out[pl.ds(2 * core + half, LANES // 2, stride=4), :] = turned[64 * q : 64 * q + 64]
+            out[pl.ds(count * core + first + half, LANES // 2, stride=2 * count), :] = turned[64 * q : 64 * q + 64]
 
     loads[0].wait()
-    spread(filt_in[...], filt_send)
+    spread(filt_in[...], filt_send, 0, 2)
     loads[1].wait()
-    spread(value_in[...].astype(F32), value_send)
+    spread(value_in[...].astype(F32), both_send, 0, 4)
     loads[2].wait()
     loads[3].wait()
-    spread(grad_in[...].astype(F32) * gate_in[...].astype(F32), grad_send)
+    spread(grad_in[...].astype(F32) * gate_in[...].astype(F32), both_send, 2, 4)
 
     pl.semaphore_wait(barrier, LANES - 1 + 3)
 
     def pair(ref, row):
         return ref.at[pl.ds(pl.multiple_of(row * 2, 2), 2)]
 
+    def four(ref, row):
+        return ref.at[pl.ds(pl.multiple_of(row * 4, 4), 4)]
+
+    def by_channel(ref, first, count):
+        return jnp.concatenate([ref[pl.ds(first + half, LANES, stride=count), :] for half in range(2)], axis=0)
+
     def to_columns(src, dst, at):
-        there = pair(dst, my_row)
+        there = four(dst, my_row)
 
         def send(peer_row, peer_col):
             pltpu.make_async_remote_copy(
-                pair(src, peer_row * 8 + peer_col), there, send_sem.at[at], recv_sem.at[at],
+                four(src, peer_row * 8 + peer_col), there, send_sem.at[at], recv_sem.at[at],
                 device_id=(seq, peer_row, peer_col), device_id_type=MESH,
             ).start()
 
-        pltpu.make_async_copy(pair(src, me), there, recv_sem.at[at]).start()
+        pltpu.make_async_copy(four(src, me), there, recv_sem.at[at]).start()
         each_peer(trow, tcol, send)
 
     def to_rows(src, dst, at, part):
@@ -242,8 +247,7 @@
     def _():
         pltpu.make_async_copy(pair(filt_send, me), filt_there, filt_sem.at[trow >> 2 & 1]).start()
 
-    to_columns(value_send, value_col, 1)
-    to_columns(grad_send, grad_col, 2)
+    to_columns(both_send, both_col, 1)
 
     def forward(column):
         spec = outer_dot(outer[0], outer[1], column)
@@ -268,17 +272,16 @@
 
     for load in loads[4:]:
         load.wait()
-    take(value_col, recv_sem.at[1])
-    value_real, value_imag = forward(value_col[...])
-    take(grad_col, recv_sem.at[2])
-    grad_real, grad_imag = forward(grad_col[...])
-    corr_col[...] = inverse(
+    take(both_col, recv_sem.at[1])
+    value_real, value_imag = forward(by_channel(both_col, 0, 4))
+    grad_real, grad_imag = forward(by_channel(both_col, 2, 4))
+    corr = inverse(
         grad_real * value_real + grad_imag * value_imag,
         grad_imag * value_real - grad_real * value_imag,
     )
     core = tcol & 1
     for half in range(2):
-        corr_parts[3 + half] = corr_col[pl.ds(half, LANES, stride=2), :]
+        corr_parts[3 + half] = corr[half * LANES : half * LANES + LANES]
     owners = [half * 2 + 1 - core for half in range(2)]
     blocks = (pl.ds(0, 16 * CUT), pl.ds(16 * CUT, LANES - 16 * CUT))
     for part, at in enumerate(blocks):
@@ -293,16 +296,22 @@
                 ).start()
 
     take(filt_col.at[pl.ds(0, 3 * quarter)], recv_sem.at[3])
-    filt_real, filt_imag = forward(filt_col[...])
-    conv_col[...] = inverse(
+    filt_real, filt_imag = forward(by_channel(filt_col, 0, 2))
+    def put(ref, result):
+        for half in range(2):
+            ref[pl.ds(half, LANES, stride=2), :] = result[half * LANES : half * LANES + LANES]
+
+    conv = inverse(
         value_real * filt_real - value_imag * filt_imag,
         value_real * filt_imag + value_imag * filt_real,
     )
+    put(conv_col, conv)
     to_rows(conv_col, conv_row, 4, 0)
-    back_col[...] = inverse(
+    back = inverse(
         grad_real * filt_real + grad_imag * filt_imag,
         grad_imag * filt_real - grad_real * filt_imag,
     )
+    put(back_col, back)
     to_rows(back_col, back_row, 5, 0)
 
     own = 3 + (seq >> 1)
@@ -354,8 +363,7 @@
     def _():
         take(filt_send.at[pl.ds(0, quarter)], send_sem.at[0])
 
-    take(value_send.at[most], send_sem.at[1])
-    take(grad_send.at[most], send_sem.at[2])
+    take(both_send.at[pl.ds(0, 4 * LANES - 4)], send_sem.at[1])
     take(filt_col.at[pl.ds(0, 3 * quarter)], send_sem.at[3])
     take(conv_col.at[most], send_sem.at[4])
     take(back_col.at[most], send_sem.at[5])
@@ -391,7 +399,8 @@
         pltpu.VMEM((2, 2 * LANES, 4 * LANES), BF16),
         pltpu.VMEM((2, LANES, LANES), F32),
     ]
-    scratch += [wide] * 11
+    double = pltpu.VMEM((4 * LANES, LANES), F32)
+    scratch += [double, wide, double, wide] + [wide] * 4
     scratch += [
         pltpu.VMEM((5, LANES, LANES), F32),
         pltpu.VMEM((LANES, LANES), F32),

time: 41.1 us -> 40.4 us (0.983)
  Pallas kernels: 40.1 us -> 39.6 us
    pallas_call x1, Pallas kernels: 39.4 us -> 38.9 us  [local(): pl.pallas_call(kernel, name='gated_conv_backward', out_shape=shapes, in_s...]
where the time goes in v4:
time: 40.4 us; the launch traced here: 40.2 us
  Pallas kernels  39.6 us (98%)
  between operations  0.64 us (2%)
    pallas_call x1, Pallas kernels, local(): pl.pallas_call(kernel, name='gated_conv_backward', out_shape=shapes, in_s...  38.9 us

profile of v4, /device:TPU:1, one launch (start us, length us, event | category | flops | bytes accessed | tf_op | source)
XLA Modules:
  0.0 40.2 jit_solution(17498455237659807985)
XLA Ops:
  0.6 38.9 %gated_conv_backward.1 = (bf16[128,256]{1,0:T(8,128)(2,1)S(1)}, bf16[128,256]{1,0:T(8,128)(2,1)S(1)}, f32[64,128]{1,0:T(8,128)S(1)}) custom-call(bf16[128,256]{1,0:T(8,128)(2,1)} %bitcast.6, bf16[128,256]{1,0:T(8,128)(2,1)} %bitcast.7, bf16[128,256]{1,0:T(8,128)(2,1)} %bitcast.8, f32[128,256]{1,0:T(8,128)} %filt_hbm.1, ...), custom_call_target="tpu_custom_call" | custom-call | tf_op jit(solution)/shard_map/gated_conv_backward/pallas_call | solution.py:417
  39.5 0.7 %store_results.1 = (bf16[128,256]{1,0:T(8,128)(2,1)}, bf16[128,256]{1,0:T(8,128)(2,1)}, f32[64,128]{1,0:T(8,128)}) custom-call(bf16[128,256]{1,0:T(8,128)(2,1)S(1)} %get-tuple-element.9.gate_in, bf16[128,256]{1,0:T(8,128)(2,1)S(1)} %get-tuple-element.10.value_in, f32[64,128]{1,0:T(8,128)S(1)} %get-tuple-element.11.filt_in), custom_call_target="tpu_custom_call" | custom-call | tf_op jit(solution)/shard_map/store_results/pallas_call | solution.py:428

commit v5 on v4

--- a/solution.py
+++ b/solution.py
@@ -83,14 +83,10 @@
     y, z, core = (tcol & 6) | (trow >> 3), trow & 7, tcol & 1
 
     def step(peer_z, carry):
-        for dy in (4, 3, 5, 2, 6, 1, 7, 0):
-            peer_y = (y + dy) & 7
+        for peer_y in range(8):
             peer_row, peer_col = ((peer_y & 1) << 3) | peer_z, (peer_y & 6) | core
             act(peer_row, peer_col ^ 1)
-            if dy:
-                act(peer_row, peer_col)
-            else:
-                pl.when(peer_z != z)(functools.partial(act, peer_row, peer_col))
+            pl.when((peer_z != z) | (y != peer_y))(functools.partial(act, peer_row, peer_col))
         return carry
 
     lax.fori_loop((0, CUT)[part], (CUT, 8)[part], step, 0)

time: 40.4 us -> 40.5 us (level)
  no operation moved by 1% of the time
where the time goes in v5:
time: 40.5 us; the launch traced here: 40.2 us
  Pallas kernels  39.6 us (98%)
  between operations  0.64 us (2%)
    pallas_call x1, Pallas kernels, local(): pl.pallas_call(kernel, name='gated_conv_backward', out_shape=shapes, in_s...  38.9 us

profile of v5, /device:TPU:1, one launch (start us, length us, event | category | flops | bytes accessed | tf_op | source)
XLA Modules:
  0.0 40.2 jit_solution(7770500789988133316)
XLA Ops:
  0.6 38.9 %gated_conv_backward.1 = (bf16[128,256]{1,0:T(8,128)(2,1)S(1)}, bf16[128,256]{1,0:T(8,128)(2,1)S(1)}, f32[64,128]{1,0:T(8,128)S(1)}) custom-call(bf16[128,256]{1,0:T(8,128)(2,1)} %bitcast.6, bf16[128,256]{1,0:T(8,128)(2,1)} %bitcast.7, bf16[128,256]{1,0:T(8,128)(2,1)} %bitcast.8, f32[128,256]{1,0:T(8,128)} %filt_hbm.1, ...), custom_call_target="tpu_custom_call" | custom-call | tf_op jit(solution)/shard_map/gated_conv_backward/pallas_call | solution.py:413
  39.5 0.7 %store_results.1 = (bf16[128,256]{1,0:T(8,128)(2,1)}, bf16[128,256]{1,0:T(8,128)(2,1)}, f32[64,128]{1,0:T(8,128)}) custom-call(bf16[128,256]{1,0:T(8,128)(2,1)S(1)} %get-tuple-element.9.gate_in, bf16[128,256]{1,0:T(8,128)(2,1)S(1)} %get-tuple-element.10.value_in, f32[64,128]{1,0:T(8,128)S(1)} %get-tuple-element.11.filt_in), custom_call_target="tpu_custom_call" | custom-call | tf_op jit(solution)/shard_map/store_results/pallas_call | solution.py:424
